TPU v7x, 32 devices: a whole 2x2x4 slice. The times are simulated.
32 devices in a mesh: groups: 2 (over y), expert: 4 (over z), role: 4 (over x, core).
Axes of the slice: x: 2, y: 2, z: 4, core: 2. Of those that a mesh axis runs over, the one named last changes fastest.
Arguments:
- tokens: bfloat16 [512, 7168], P(('groups', 'expert'), 'role'), parts along dimension 0, may hold values from -6 to 6
- routes: int32 [512, 8], P(('groups', 'expert')), parts along dimension 0, may hold values from 0 to 31, all different within a row; in each aligned block of 64 rows (0 to 63, 64 to 127, ...) at most 32 rows name the same one
- route_weights: float32 [512, 8], P(('groups', 'expert')), parts along dimension 0, may hold values from 0.1 to 1
- w_gate: bfloat16 [32, 7168, 1024], P('expert', 'role'), may hold values from -0.0625 to 0.0625
- w_up: bfloat16 [32, 7168, 1024], P('expert', 'role'), may hold values from -0.0625 to 0.0625
- w_down: bfloat16 [32, 1024, 7168], P('expert', None, 'role'), may hold values from -0.1875 to 0.1875
- latent: bfloat16 [512, 576], P(('groups', 'expert', 'role')), parts along dimension 0, may hold values from -400 to 400
- norm_gain: float32 [512], replicated, may hold values from 0.1 to 1.9
- prompt_lengths: int32 [16], P('groups'), parts along dimension 0, may hold values from 1 to 128, 256 in all
- span_offsets: int32 [16], P('groups'), parts along dimension 0, may hold values from 0 to 16383
- slot_source: int32 [32], P(('groups', 'expert', 'role')), parts along dimension 0, may hold values from 0 to 15, each once
Outputs:
- mixed_out: bfloat16 [512, 7168], P(('groups', 'expert'), 'role'), parts along dimension 0
- decode_cache: bfloat16 [32, 9216], P(('groups', 'expert', 'role')), parts along dimension 0
There are 2 independent parts, one for each index of `groups`. A program takes and returns all parts, laid end to end along the dimension named above; an argument that names none is the same for every part. Nothing has to cross between parts.
Inputs may be any that keep to these rules, and one draw needn't show every extreme that they name: `routes`: within the 64 rows of one expert index no expert is named by more than 32 pairs, a bound that some block reaches; a row names 8 different experts. `slot_source`: each block number appears once.
All inputs are finite; a program needn't handle non-finite values.
Results may differ from a plain program's by a relative error of at most 0.0058.
Values may be sent and summed in bfloat16 or wider, within the bound.
A program may use at most 256 MiB of HBM per device.

v0:
```python
import math

import jax
import jax.numpy as jnp
from jax import lax
from jax.sharding import PartitionSpec as P

LAT = 512
ROPE = 64
EXPERTS = 32
BLK = 16
MOST = 32


def token_positions(token_index, prompt_lengths, span_offsets):
    starts = jnp.cumsum(prompt_lengths) - prompt_lengths
    inside = (token_index[:, None] >= starts[None, :]) & (
        token_index[:, None] < (starts + prompt_lengths)[None, :]
    )
    placed = span_offsets[None, :] + token_index[:, None] - starts[None, :]
    return jnp.sum(jnp.where(inside, placed, 0), axis=1).astype(jnp.float32)


def latent_rows(latent, norm_gain, positions_f):
    latent_f = latent.astype(jnp.float32)
    compressed = latent_f[:, :LAT]
    rope_part = latent_f[:, LAT:]
    normed = (
        compressed
        * lax.rsqrt(jnp.mean(compressed * compressed, axis=1, keepdims=True) + 1e-06)
        * norm_gain[None, :]
    )
    half_rope = ROPE // 2
    inverse_freq = jnp.exp(
        jnp.arange(half_rope, dtype=jnp.float32) * (-2.0 * math.log(10000.0) / ROPE)
    )
    angles = positions_f[:, None] * inverse_freq[None, :]
    cosine = jnp.cos(angles)
    sine_part = jnp.sin(angles)
    first_half = rope_part[:, :half_rope]
    second_half = rope_part[:, half_rope:]
    rotated = jnp.concatenate(
        [
            first_half * cosine - second_half * sine_part,
            second_half * cosine + first_half * sine_part,
        ],
        axis=1,
    )
    return jnp.concatenate([normed, rotated], axis=1).astype(jnp.bfloat16)


def local(
    tokens,
    routes,
    route_weights,
    w_gate,
    w_up,
    w_down,
    latent,
    norm_gain,
    prompt_lengths,
    span_offsets,
    slot_source,
):
    experts_here = w_gate.shape[0]
    token_count = routes.shape[0]
    route_count = routes.shape[1]
    feat_width = tokens.shape[1]
    expert_devices = lax.axis_size("expert")
    flat_routes = routes.reshape(-1)
    onehot = (flat_routes[:, None] == jnp.arange(EXPERTS, dtype=jnp.int32)[None, :]).astype(
        jnp.int32
    )
    earlier = jnp.cumsum(onehot, axis=0) - onehot
    dest_row = flat_routes * MOST + jnp.sum(earlier * onehot, axis=1)
    pair_tok = jnp.arange(token_count * route_count, dtype=jnp.int32) // route_count
    slot_table = jnp.full((EXPERTS * MOST,), token_count, jnp.int32).at[dest_row].set(pair_tok)
    padded = jnp.concatenate([tokens, jnp.zeros((1, feat_width), tokens.dtype)], axis=0)
    outgoing = padded[slot_table]
    incoming = lax.all_to_all(outgoing, "expert", split_axis=0, concat_axis=0, tiled=True)
    grouped = incoming.reshape(expert_devices, experts_here, MOST, feat_width)
    gate_part = jnp.einsum("secd,edf->secf", grouped, w_gate, preferred_element_type=jnp.float32)
    up_part = jnp.einsum("secd,edf->secf", grouped, w_up, preferred_element_type=jnp.float32)
    gate_act, up_act = lax.psum((gate_part, up_part), "role")
    hidden = (jax.nn.silu(gate_act) * up_act).astype(jnp.bfloat16)
    result = jnp.einsum(
        "secf,efd->secd", hidden, w_down, preferred_element_type=jnp.float32
    ).astype(jnp.bfloat16)
    returned = lax.all_to_all(
        result.reshape(expert_devices * experts_here * MOST, feat_width),
        "expert",
        split_axis=0,
        concat_axis=0,
        tiled=True,
    )
    picked = returned[dest_row].reshape(token_count, route_count, feat_width)
    mixed_out = jnp.sum(picked * route_weights[:, :, None], axis=1).astype(jnp.bfloat16)
    latent_count = latent.shape[0]
    token_index = lax.axis_index(("expert", "role")) * latent_count + jnp.arange(
        latent_count, dtype=jnp.int32
    )
    positions_f = token_positions(token_index, prompt_lengths, span_offsets)
    cache_rows = latent_rows(latent, norm_gain, positions_f)
    blocks = cache_rows.reshape(latent_count // BLK, BLK * latent.shape[1])
    shard_piece = lax.all_gather(blocks, ("expert", "role"), axis=0, tiled=True)
    block_ids = jnp.arange(shard_piece.shape[0], dtype=jnp.int32)
    picker = (slot_source[:, None] == block_ids[None, :]).astype(jnp.bfloat16)
    decode_cache = jnp.dot(picker, shard_piece, preferred_element_type=jnp.float32).astype(
        jnp.bfloat16
    )
    return (mixed_out, decode_cache)


def solution(mesh):
    in_specs = (
        P(("groups", "expert"), "role"),
        P(("groups", "expert"), None),
        P(("groups", "expert"), None),
        P("expert", "role", None),
        P("expert", "role", None),
        P("expert", None, "role"),
        P(("groups", "expert", "role"), None),
        P(),
        P("groups"),
        P("groups"),
        P(("groups", "expert", "role")),
    )
    out_specs = (P(("groups", "expert"), "role"), P(("groups", "expert", "role"), None))
    return jax.shard_map(local, mesh=mesh, in_specs=in_specs, out_specs=out_specs, check_vma=False)
```

profile of v0, /device:TPU:0, one launch (start us, length us, event | category | flops | bytes accessed | tf_op | source)
XLA Modules:
  0.0 424.5 jit_solution(17309629718776356739)
XLA Ops:
  7.2 0.0 all-reduce.4.cloned.1.call-start
  7.2 0.8 copy.30
  8.0 0.1 eq.42
  8.1 0.1 eq.38
  8.2 0.7 broadcast_multiply_fusion
  8.9 1.2 reduce-window.18
  10.0 0.2 slice_reduce_fusion
  10.3 0.1 copy.29
  10.4 0.1 mul.96
  10.5 0.1 fusion.31
  10.6 2.4 scatter_custom_fusion
  13.1 1.0 concatenate.7
  14.0 5.8 %gather_fusion = bf16[1024,1792]{1,0:T(8,128)(2,1)} fusion(bf16[65,1792]{1,0:T(8,128)(2,1)S(1)} %concatenate.7, s32[1024]{0:T(1024)S(1)} %fusion.41), kind=kCustom, calls=%fused_computation | custom fusion | bytes 7344128 | tf_op jit(solution)/shard_map/gather | solution.py:79
  19.9 88.2 %all_to_all.21 = bf16[4,256,1792]{2,1,0:T(8,128)(2,1)S(1)} all-to-all(bf16[4,256,1792]{2,1,0:T(8,128)(2,1)} %bitcast.71), channel_id=1, replica_groups=mesh['groups'=2,'expert'=4,'role'=4] {'expert'}, dimensions={0} | all-to-all | bytes 7340032 | tf_op jit(solution)/shard_map/all_to_all | solution.py:80
  108.1 15.5 %fusion.15 = f32[4,8,32,1024]{3,2,0,1:T(8,128)} fusion(bf16[8,1792,1024]{2,1,0:T(8,128)(2,1)} %param.14, bf16[4,8,32,1792]{3,2,1,0:T(8,128)(2,1)S(1)} %bitcast.69), kind=kOutput, calls=%fused_computation.16 | convolution fusion | flops 3758096384 | bytes 37224448 | tf_op jit(solution)/shard_map/secd,edf->secf/dot_general | solution.py:82
  123.6 15.5 %fusion.20 = f32[4,8,32,1024]{3,2,0,1:T(8,128)} fusion(bf16[8,1792,1024]{2,1,0:T(8,128)(2,1)} %param.15, bf16[4,8,32,1792]{3,2,1,0:T(8,128)(2,1)S(1)} %bitcast.70), kind=kOutput, calls=%fused_computation.17 | convolution fusion | flops 3758096384 | bytes 37224448 | tf_op jit(solution)/shard_map/secd,edf->secf/dot_general | solution.py:83
  139.1 0.0 all-reduce.4.cloned.1.call-update
  139.1 152.8 %all-reduce.4.cloned.1.call-done = (f32[4,8,32,1024]{3,2,0,1:T(8,128)}, f32[4,8,32,1024]{3,2,0,1:T(8,128)}) async-done(((f32[4,8,32,1024]{3,2,0,1:T(8,128)}, f32[4,8,32,1024]{3,2,0,1:T(8,128)}), (f32[4,8,32,1024]{3,2,0,1:T(8,128)}, f32[4,8,32,1024]{3,2,0,1:T(8,128)})) %all-reduce.4.cloned.1.call-update) | async-done | bytes 8388624 | tf_op jit(solution)/shard_map/psum | solution.py:84
  291.9 16.5 %fusion.10 = bf16[4,8,32,1792]{3,2,0,1:T(8,128)(2,1)} fusion(bf16[8,1024,1792]{2,1,0:T(8,128)(2,1)} %param.16, f32[4,8,32,1024]{3,2,0,1:T(8,128)} %get-tuple-element.2, f32[4,8,32,1024]{3,2,0,1:T(8,128)} %get-tuple-element.3), kind=kOutput, calls=%fused_computation.13 | convolution fusion | flops 3766222848 | bytes 41418752 | tf_op jit(solution)/shard_map/secf,efd->secd/dot_general | solution.py:86
  308.3 4.1 copy.35
  312.5 0.0 copy-start.1
  312.5 0.0 copy-start.4
  312.5 0.0 copy-start.3
  312.5 0.0 copy-start
  312.5 0.0 copy-start.2
  312.5 4.9 %all-to-all-start.1 = ((bf16[4,256,1792]{2,1,0:T(8,128)(2,1)}), bf16[4,256,1792]{2,1,0:T(8,128)(2,1)}, u32[]{:S(2)}, u32[]{:S(2)}) async-start(bf16[4,256,1792]{2,1,0:T(8,128)(2,1)} %bitcast.72), calls=%async_computation.1 | async-start | bytes 7340032 | tf_op jit(solution)/shard_map/all_to_all | solution.py:89
  317.4 0.0 copy-done.1
  317.4 0.1 copy.36
  317.5 0.0 copy-done.4
  317.5 0.2 reduce-window.20
  317.7 0.0 copy-done.3
  317.7 0.1 select_reduce_fusion
  317.8 0.0 copy-done
  317.8 0.1 multiply_reduce_fusion
  317.9 0.1 fusion.38
  318.1 0.0 copy-done.2
  318.1 0.1 multiply_convert_fusion.2
  318.2 0.1 pad_maximum_fusion
  318.2 0.1 reshape.161
  319.0 89.1 %all-gather = bf16[16,1,9216]{2,1,0:T(2,128)(2,1)S(1)} all-gather(bf16[1,1,9216]{2,1,0:T(2,128)(2,1)S(1)} %reshape.161), channel_id=1, replica_groups=mesh['groups'=2,'expert'=4,'role'=4] {'expert','role'}, dimensions={0}, use_global_device_ids=true | all-gather | bytes 313344 | tf_op jit(solution)/shard_map/all_gather | solution.py:105
  408.1 0.2 fusion.26
  408.3 0.6 convert_element_type.65
  408.9 0.0 all-to-all-done.1
  408.9 6.5 %gather_fusion.1 = bf16[512,1792]{1,0:T(8,128)(2,1)S(1)} fusion(bf16[1024,1792]{1,0:T(8,128)(2,1)} %bitcast.15, s32[1024]{0:T(1024)S(1)} %pad_clamp_fusion), kind=kCustom, calls=%fused_computation.1 | custom fusion | bytes 3672064 | tf_op jit(solution)/shard_map/gather | solution.py:96
  415.4 2.3 fusion.9
  (14 shorter events, 0.1 us)
Async XLA Ops:
  7.2 284.7 %all-reduce.4.cloned.1.call-start = ((), (), s32[]{:S(2)}) async-start(), calls=%async_computation.2 | async-start | bytes 16777216 | tf_op jit(solution)/shard_map/psum | solution.py:84
  312.5 4.9 %copy-start.1 = (f32[64,8]{0,1:T(8,128)S(1)}, f32[64,8]{0,1:T(8,128)}, u32[]{:S(2)}) copy-start(f32[64,8]{0,1:T(8,128)} %param.13) | copy-start | bytes 6148
  312.5 5.0 %copy-start.4 = (s32[8]{0:T(128)S(1)}, s32[8]{0:T(128)}, u32[]{:S(2)}) copy-start(s32[8]{0:T(128)} %param.19) | copy-start | bytes 100
  312.5 5.2 %copy-start.3 = (s32[8]{0:T(128)S(1)}, s32[8]{0:T(128)}, u32[]{:S(2)}) copy-start(s32[8]{0:T(128)} %param.20) | copy-start | bytes 100
  312.5 5.3 %copy-start = (bf16[16,576]{1,0:T(8,128)(2,1)S(1)}, bf16[16,576]{1,0:T(8,128)(2,1)}, u32[]{:S(2)}) copy-start(bf16[16,576]{1,0:T(8,128)(2,1)} %param.17) | copy-start | bytes 55300
  312.5 5.6 %copy-start.2 = (f32[512]{0:T(512)S(1)}, f32[512]{0:T(512)}, u32[]{:S(2)}) copy-start(f32[512]{0:T(512)} %param.18) | copy-start | bytes 6148
  312.5 96.4 %all-to-all-start.1 = ((bf16[4,256,1792]{2,1,0:T(8,128)(2,1)}), bf16[4,256,1792]{2,1,0:T(8,128)(2,1)}, u32[]{:S(2)}, u32[]{:S(2)}) async-start(bf16[4,256,1792]{2,1,0:T(8,128)(2,1)} %bitcast.72), calls=%async_computation.1 | async-start | bytes 7340032 | tf_op jit(solution)/shard_map/all_to_all | solution.py:89
Sparse Core Ops, SparseCore 0:
  139.2 152.5 all-reduce.3
where the time goes:
time: 427 us; the launch traced here: 425 us
  blocking collectives  177 us (41%)
  waiting for transfers between devices  153 us (36%)
  matrix products  47.7 us (11%)
  local copies, waits for them, and re-layouts  22 us (5%)
  between operations  14.8 us (3%)
  other arithmetic  5.04 us (1%)
  starting transfers between devices  4.92 us (1%)
    psum x1, waiting for transfers between devices, local(): gate_act, up_act = lax.psum((gate_part, up_part), 'role')  153 us
    all_gather x1, blocking collectives, local(): shard_piece = lax.all_gather(blocks, ('expert', 'role'), axis=0, tiled=True)  89.1 us
    all_to_all x1, blocking collectives, local(): lax.all_to_all(outgoing, 'expert', split_axis=0, concat_axis=0, tiled=True)  88.2 us
    dot_general x1, matrix products, local(): jnp.einsum('secf,efd->secd', hidden, w_down, preferred_element_type=jnp.f...  16.5 us
    dot_general x1, matrix products, local(): jnp.einsum('secd,edf->secf', grouped, w_up, preferred_element_type=jnp.fl...  15.5 us
    dot_general x1, matrix products, local(): jnp.einsum('secd,edf->secf', grouped, w_gate, preferred_element_type=jnp....  15.5 us
  transfers between devices with their start and end apart: 2, of which 1 were waited for; matrix products, arithmetic and copies ran while one was open for 0% of the time, Pallas kernels for 0%

commit v1 on v0

--- a/solution.py
+++ b/solution.py
@@ -1,8 +1,11 @@
+import functools
 import math
 
 import jax
 import jax.numpy as jnp
 from jax import lax
+from jax.experimental import pallas as pl
+from jax.experimental.pallas import tpu as pltpu
 from jax.sharding import PartitionSpec as P
 
 LAT = 512
@@ -49,19 +52,349 @@
     return jnp.concatenate([normed, rotated], axis=1).astype(jnp.bfloat16)
 
 
-def local(
-    tokens,
-    routes,
-    route_weights,
-    w_gate,
-    w_up,
-    w_down,
-    latent,
-    norm_gain,
-    prompt_lengths,
-    span_offsets,
-    slot_source,
+GATE_SLOTS = 4
+DOWN_SLOTS = 5
+VMEM_LIMIT = 62 * 1024 * 1024
+
+
+def fits_kernel(tokens, w_gate):
+    return (
+        lax.axis_size("role") == 4
+        and lax.axis_size("expert") * MOST <= 128
+        and w_gate.shape[0] >= DOWN_SLOTS
+    )
+
+
+def moe_kernel(
+    sources,
+    tok_ref,
+    routes_ref,
+    rw_ref,
+    wg_ref,
+    wu_ref,
+    wd_ref,
+    out_ref,
+    tok_all,
+    info_all,
+    info_mine,
+    info_row,
+    wslots,
+    dslots,
+    xbuf,
+    own,
+    send1,
+    recv1,
+    send2,
+    recv2,
+    hid,
+    hs,
+    acc,
+    psend,
+    precv,
+    wsem,
+    dsem,
+    tok_send,
+    tok_recv,
+    info_send,
+    info_recv,
+    s1_send,
+    s1_recv,
+    s2_send,
+    s2_recv,
+    h_send,
+    h_recv,
+    p_send,
+    p_recv,
 ):
+    z = lax.axis_index("expert")
+    role = lax.axis_index("role")
+    chip = lax.div(role, 2)
+    core = lax.rem(role, 2)
+    core_peer = {"role": chip * 2 + (1 - core)}
+    chip_peer = {"role": (1 - chip) * 2 + core}
+    experts = wg_ref.shape[0]
+    count = tok_ref.shape[0]
+    width = tok_ref.shape[1]
+    ff = wg_ref.shape[2]
+    half = ff // 2
+    quarter = ff // 4
+    slots = sources * MOST
+    peers = [{"expert": lax.rem(z + d, sources)} for d in range(1, sources)]
+
+    def weight_copy(ref, which, e):
+        slot = lax.rem(2 * e + which, GATE_SLOTS)
+        return pltpu.make_async_copy(ref.at[e], wslots.at[slot], wsem.at[slot])
+
+    def down_copy(e):
+        slot = lax.rem(e, DOWN_SLOTS)
+        return pltpu.make_async_copy(wd_ref.at[e], dslots.at[slot], dsem.at[slot])
+
+    for e in range(GATE_SLOTS // 2):
+        weight_copy(wg_ref, 0, e).start()
+        weight_copy(wu_ref, 1, e).start()
+    for e in range(DOWN_SLOTS):
+        down_copy(e).start()
+
+    barrier = pltpu.get_barrier_semaphore()
+    everyone = peers + [core_peer, chip_peer]
+    for peer in everyone:
+        pl.semaphore_signal(barrier, inc=1, device_id=peer, device_id_type=pl.DeviceIdType.MESH)
+    pl.semaphore_wait(barrier, len(everyone))
+
+    def remote(src, dst, send_sem, recv_sem, peer):
+        return pltpu.make_async_remote_copy(
+            src_ref=src,
+            dst_ref=dst,
+            send_sem=send_sem,
+            recv_sem=recv_sem,
+            device_id=peer,
+            device_id_type=pl.DeviceIdType.MESH,
+        )
+
+    def token_copy(d):
+        return remote(
+            tok_ref, tok_all.at[pl.ds(d * count, count)], tok_send.at[d], tok_recv.at[d], peers[d - 1]
+        )
+
+    def info_copy(d):
+        return remote(info_mine, info_all.at[d], info_send.at[d], info_recv.at[d], peers[d - 1])
+
+    expert_id = lax.broadcasted_iota(jnp.int32, (EXPERTS, count), 0)
+    member = jnp.zeros((EXPERTS, count), jnp.float32)
+    weight = jnp.zeros((EXPERTS, count), jnp.float32)
+    for k in range(routes_ref.shape[0]):
+        hit = routes_ref[k : k + 1, :] == expert_id
+        member = member + jnp.where(hit, 1.0, 0.0)
+        weight = weight + jnp.where(hit, rw_ref[k : k + 1, :], 0.0)
+    before = jnp.where(
+        lax.broadcasted_iota(jnp.int32, (count, count), 0)
+        < lax.broadcasted_iota(jnp.int32, (count, count), 1),
+        1.0,
+        0.0,
+    ).astype(jnp.bfloat16)
+    rank = jnp.dot(member.astype(jnp.bfloat16), before, preferred_element_type=jnp.float32)
+    info_mine[0:EXPERTS, 0:count] = jnp.where(member > 0.5, rank, -1000.0)
+    info_mine[EXPERTS : 2 * EXPERTS, 0:count] = weight
+    info_mine[:, count:] = jnp.zeros((2 * EXPERTS, info_mine.shape[1] - count), jnp.float32)
+
+    for d in range(1, sources):
+        info_copy(d).start()
+    for d in range(1, sources):
+        token_copy(d).start()
+    tok_all[0:count, :] = tok_ref[...]
+    for d in range(1, sources):
+        info_copy(d).wait_recv()
+    rows = [info_mine[:, 0:count]] + [info_all[d, :, 0:count] for d in range(1, sources)]
+    rows = [r + jnp.where(
+        lax.broadcasted_iota(jnp.int32, r.shape, 0) < EXPERTS, float(d * MOST), 0.0
+    ) for d, r in enumerate(rows)]
+    info_row[...] = jnp.concatenate(rows, axis=1)
+    for d in range(1, sources):
+        token_copy(d).wait_recv()
+
+    slot_id = lax.broadcasted_iota(jnp.int32, (slots, sources * count), 0).astype(jnp.float32)
+
+    def placing(e):
+        row = info_row[pl.ds(z * experts + e, 1), :]
+        return row == slot_id
+
+    def core_copy(e):
+        return remote(send1.at[e], recv1.at[e], s1_send.at[e], s1_recv.at[e], core_peer)
+
+    def chip_copy(e):
+        return remote(send2.at[e], recv2.at[e], s2_send.at[e], s2_recv.at[e], chip_peer)
+
+    mine = core * 2 + chip
+    theirs = core * 2 + (1 - chip)
+
+    def hid_copy(e, kind):
+        q = mine if kind < 2 else theirs
+        peer = chip_peer if kind == 0 else core_peer
+        return remote(hid.at[e, q], hid.at[e, q], h_send.at[e, kind], h_recv.at[e, kind], peer)
+
+    def project(e):
+        weight_copy(wg_ref, 0, e).wait()
+        weight_copy(wu_ref, 1, e).wait()
+        one_hot = jnp.where(placing(e), 1.0, 0.0).astype(jnp.bfloat16)
+        xbuf[...] = jnp.dot(
+            one_hot, tok_all[...], preferred_element_type=jnp.float32
+        ).astype(jnp.bfloat16)
+        gate_slot = lax.rem(2 * e, GATE_SLOTS)
+        for where_to, part in ((send1, 1 - core), (own, core)):
+            cols = pl.ds(pl.multiple_of(part * half, half), half)
+            for which in range(2):
+                where_to[e, :, which * half : (which + 1) * half] = jnp.dot(
+                    xbuf[...],
+                    wslots[gate_slot + which, :, cols],
+                    preferred_element_type=jnp.float32,
+                )
+            if where_to is send1:
+                core_copy(e).start()
+
+        @pl.when(e + GATE_SLOTS // 2 < experts)
+        def _():
+            weight_copy(wg_ref, 0, e + GATE_SLOTS // 2).start()
+            weight_copy(wu_ref, 1, e + GATE_SLOTS // 2).start()
+
+    def add_core(e):
+        core_copy(e).wait_recv()
+        for which in range(2):
+            keep = pl.ds(pl.multiple_of(which * half + chip * quarter, quarter), quarter)
+            give = pl.ds(pl.multiple_of(which * half + (1 - chip) * quarter, quarter), quarter)
+            send2[e, :, which * quarter : (which + 1) * quarter] = (
+                own[e, :, give] + recv1[e, :, give]
+            ).astype(jnp.bfloat16)
+        chip_copy(e).start()
+        for which in range(2):
+            keep = pl.ds(pl.multiple_of(which * half + chip * quarter, quarter), quarter)
+            own[e, :, keep] = own[e, :, keep] + recv1[e, :, keep]
+
+    def activate(e):
+        chip_copy(e).wait_recv()
+        sums = []
+        for which in range(2):
+            keep = pl.ds(pl.multiple_of(which * half + chip * quarter, quarter), quarter)
+            got = recv2[e, :, which * quarter : (which + 1) * quarter]
+            sums.append(own[e, :, keep] + got.astype(jnp.float32))
+        w_row = info_row[pl.ds(EXPERTS + z * experts + e, 1), :]
+        w_slot = jnp.sum(jnp.where(placing(e), w_row, 0.0), axis=1, keepdims=True)
+        hid[e, mine] = (jax.nn.silu(sums[0]) * sums[1] * w_slot).astype(jnp.bfloat16)
+        hid_copy(e, 0).start()
+        hid_copy(e, 1).start()
+
+    def forward(e):
+        hid_copy(e, 0).wait_recv()
+        hid_copy(e, 2).start()
+
+    def finish(e):
+        hid_copy(e, 1).wait_recv()
+        hid_copy(e, 2).wait_recv()
+        one_hot = jnp.where(placing(e), 1.0, 0.0).astype(jnp.bfloat16)
+        for q in range(4):
+            hs[:, q * quarter : (q + 1) * quarter] = lax.dot_general(
+                one_hot,
+                hid[e, q],
+                (((0,), (0,)), ((), ())),
+                preferred_element_type=jnp.float32,
+            ).astype(jnp.bfloat16)
+        down_copy(e).wait()
+        slot = lax.rem(e, DOWN_SLOTS)
+
+        def columns(j, carry):
+            cols = pl.ds(pl.multiple_of(j * 256, 256), 256)
+            acc[:, cols] += jnp.dot(
+                hs[...], dslots[slot, :, cols], preferred_element_type=jnp.float32
+            )
+            return carry
+
+        lax.fori_loop(0, width // 256, columns, 0)
+
+        @pl.when(e + DOWN_SLOTS < experts)
+        def _():
+            down_copy(e + DOWN_SLOTS).start()
+
+    acc[...] = jnp.zeros_like(acc)
+
+    def step(i, carry):
+        for lag, stage in enumerate((project, add_core, activate, forward, finish)):
+
+            @pl.when((i >= lag) & (i - lag < experts))
+            def _():
+                stage(i - lag)
+
+        return carry
+
+    lax.fori_loop(0, experts + 4, step, 0)
+
+    def back_copy(d):
+        return remote(
+            psend.at[d], precv.at[d], p_send.at[d], p_recv.at[d], {"expert": lax.rem(z + sources - d, sources)}
+        )
+
+    for d in range(1, sources):
+        psend[d] = acc[d * count : (d + 1) * count, :].astype(jnp.bfloat16)
+        back_copy(d).start()
+    total = acc[0:count, :]
+    for d in range(1, sources):
+        back_copy(d).wait_recv()
+        total = total + precv[d].astype(jnp.float32)
+    out_ref[...] = total.astype(out_ref.dtype)
+
+    for d in range(1, sources):
+        info_copy(d).wait_send()
+        token_copy(d).wait_send()
+        back_copy(d).wait_send()
+
+    def drain(e, carry):
+        core_copy(e).wait_send()
+        chip_copy(e).wait_send()
+        for kind in range(3):
+            hid_copy(e, kind).wait_send()
+        return carry
+
+    lax.fori_loop(0, experts, drain, 0)
+
+
+def experts_kernel(tokens, routes, route_weights, w_gate, w_up, w_down):
+    sources = lax.axis_size("expert")
+    count, width = tokens.shape
+    experts, _, ff = w_gate.shape
+    slots = sources * MOST
+    half, quarter = ff // 2, ff // 4
+    bf16, f32 = jnp.bfloat16, jnp.float32
+    vmem = pl.BlockSpec(memory_space=pltpu.VMEM)
+    hbm = pl.BlockSpec(memory_space=pl.ANY)
+    dma = pltpu.SemaphoreType.DMA
+    return pl.pallas_call(
+        functools.partial(moe_kernel, sources),
+        out_shape=jax.ShapeDtypeStruct((count, width), bf16),
+        in_specs=[vmem, vmem, vmem, hbm, hbm, hbm],
+        out_specs=vmem,
+        scratch_shapes=[
+            pltpu.VMEM((sources * count, width), bf16),
+            pltpu.VMEM((sources, 2 * EXPERTS, 128), f32),
+            pltpu.VMEM((2 * EXPERTS, 128), f32),
+            pltpu.VMEM((2 * EXPERTS, sources * count), f32),
+            pltpu.VMEM((GATE_SLOTS, width, ff), bf16),
+            pltpu.VMEM((DOWN_SLOTS, ff, width), bf16),
+            pltpu.VMEM((slots, width), bf16),
+            pltpu.VMEM((experts, slots, ff), f32),
+            pltpu.VMEM((experts, slots, ff), f32),
+            pltpu.VMEM((experts, slots, ff), f32),
+            pltpu.VMEM((experts, slots, half), bf16),
+            pltpu.VMEM((experts, slots, half), bf16),
+            pltpu.VMEM((experts, 4, slots, quarter), bf16),
+            pltpu.VMEM((sources * count, ff), bf16),
+            pltpu.VMEM((sources * count, width), f32),
+            pltpu.VMEM((sources, count, width), bf16),
+            pltpu.VMEM((sources, count, width), bf16),
+            dma((GATE_SLOTS,)),
+            dma((DOWN_SLOTS,)),
+            dma((sources,)),
+            dma((sources,)),
+            dma((sources,)),
+            dma((sources,)),
+            dma((experts,)),
+            dma((experts,)),
+            dma((experts,)),
+            dma((experts,)),
+            dma((experts, 3)),
+            dma((experts, 3)),
+            dma((sources,)),
+            dma((sources,)),
+        ],
+        compiler_params=pltpu.CompilerParams(
+            collective_id=0, has_side_effects=True, vmem_limit_bytes=VMEM_LIMIT
+        ),
+        cost_estimate=pl.CostEstimate(
+            flops=8 * experts * slots * width * ff,
+            bytes_accessed=6 * experts * width * ff,
+            transcendentals=0,
+        ),
+    )(tokens, routes.T, route_weights.T, w_gate, w_up, w_down)
+
+
+def experts_plain(tokens, routes, route_weights, w_gate, w_up, w_down):
     experts_here = w_gate.shape[0]
     token_count = routes.shape[0]
     route_count = routes.shape[1]
@@ -95,6 +428,10 @@
     )
     picked = returned[dest_row].reshape(token_count, route_count, feat_width)
     mixed_out = jnp.sum(picked * route_weights[:, :, None], axis=1).astype(jnp.bfloat16)
+    return mixed_out
+
+
+def decode_blocks(latent, norm_gain, prompt_lengths, span_offsets, slot_source):
     latent_count = latent.shape[0]
     token_index = lax.axis_index(("expert", "role")) * latent_count + jnp.arange(
         latent_count, dtype=jnp.int32
@@ -108,6 +445,27 @@
     decode_cache = jnp.dot(picker, shard_piece, preferred_element_type=jnp.float32).astype(
         jnp.bfloat16
     )
+    return decode_cache
+
+
+def local(
+    tokens,
+    routes,
+    route_weights,
+    w_gate,
+    w_up,
+    w_down,
+    latent,
+    norm_gain,
+    prompt_lengths,
+    span_offsets,
+    slot_source,
+):
+    decode_cache = decode_blocks(latent, norm_gain, prompt_lengths, span_offsets, slot_source)
+    if fits_kernel(tokens, w_gate):
+        mixed_out = experts_kernel(tokens, routes, route_weights, w_gate, w_up, w_down)
+    else:
+        mixed_out = experts_plain(tokens, routes, route_weights, w_gate, w_up, w_down)
     return (mixed_out, decode_cache)
 
 

time: 427 us -> 125 us (0.29)
  waiting for transfers between devices: 153 us -> 0 us
  blocking collectives: 177 us -> 24.8 us
  Pallas kernels: 0 us -> 92.2 us
  matrix products: 47.7 us -> 0.2 us
  local copies, waits for them, and re-layouts: 22 us -> 2.39 us
  between operations: 14.8 us -> 1.32 us
  starting transfers between devices: 4.92 us -> 0 us
    psum x1 -> x0, waiting for transfers between devices: 153 us -> none  [local(): gate_act, up_act = lax.psum((gate_part, up_part), 'role')]
    pallas_call x0 -> x1, Pallas kernels: none -> 92.2 us  [experts_kernel(): pl.pallas_call(functools.partial(moe_kernel, sources), out_shape=jax.Shap...]
    all_to_all x1 -> x0, blocking collectives: 88.2 us -> none  [local(): lax.all_to_all(outgoing, 'expert', split_axis=0, concat_axis=0, tiled=True)]
    all_gather x1, blocking collectives: 89.1 us -> 24.8 us  [decode_blocks(): shard_piece = lax.all_gather(blocks, ('expert', 'role'), axis=0, tiled=True)]
    dot_general x4 -> x1, matrix products: 47.7 us -> 0.2 us  [decode_blocks(): jnp.dot(picker, shard_piece, preferred_element_type=jnp.float32)]
    gather x2 -> x0, local copies, waits for them, and re-layouts: 12.3 us -> none  [the longest x1 6.45 us: local(): picked = returned[dest_row].reshape(token_count, route_count, feat_width)]
    all_to_all x1 -> x0, starting transfers between devices: 4.88 us -> none  [local(): lax.all_to_all(result.reshape(expert_devices * experts_here * MOST, feat_...]
  transfers between devices with their start and end apart: 2 -> 0, of which waited for: 1 -> 0; matrix products, arithmetic and copies ran while one was open for 0% -> 0% of each run, Pallas kernels for 0% -> 0%
where the time goes in v1:
time: 125 us
  Pallas kernels  92.2 us (74%)
  blocking collectives  24.8 us (20%)
  other arithmetic  4.08 us (3%)
  local copies, waits for them, and re-layouts  2.39 us (2%)
  between operations  1.32 us (1%)
    pallas_call x1, Pallas kernels, experts_kernel(): pl.pallas_call(functools.partial(moe_kernel, sources), out_shape=jax.Shap...  92.2 us
    all_gather x1, blocking collectives, decode_blocks(): shard_piece = lax.all_gather(blocks, ('expert', 'role'), axis=0, tiled=True)  24.8 us

profile of v1, /device:TPU:0, one launch (start us, length us, event | category | flops | bytes accessed | tf_op | source)
XLA Modules:
  0.0 125.0 jit_solution(14333926504074020035)
XLA Ops:
  0.6 0.8 reduce-window.8
  1.5 0.7 bitcast_subtract_fusion
  2.1 0.7 select_reduce_fusion
  2.9 0.7 convert_element_type.28
  3.6 0.1 fusion.8
  3.8 0.1 multiply_reduce_fusion
  3.9 0.8 multiply_convert_fusion
  4.6 0.1 pad_maximum_fusion
  4.7 0.1 reshape.73
  4.8 24.8 %all-gather = bf16[16,1,9216]{2,1,0:T(2,128)(2,1)S(1)} all-gather(bf16[1,1,9216]{2,1,0:T(2,128)(2,1)S(1)} %reshape.73), channel_id=1, replica_groups=mesh['groups'=2,'expert'=4,'role'=4] {'expert','role'}, dimensions={0}, use_global_device_ids=true | all-gather | bytes 313344 | tf_op jit(solution)/shard_map/all_gather | solution.py:442
  30.3 0.2 fusion
  30.5 0.6 convert_element_type.32
  31.2 92.2 %shard_map.122 = bf16[64,1792]{1,0:T(8,128)(2,1)} custom-call(bf16[64,1792]{1,0:T(8,128)(2,1)} %tok_ref.1, s32[8,64]{1,0:T(8,128)} %bitcast.15, f32[8,64]{1,0:T(8,128)} %bitcast.16, bf16[8,1792,1024]{2,1,0:T(8,128)(2,1)} %wg_ref.1, bf16[8,1792,1024]{2,1,0:T(8,128)(2,1)} %wu_ref.1, bf16[8,1024,1792]{2,1,0:T(8,128)(2,1)} %wd_ref.1), custom_call_target="tpu_custom_call" | custom-call | flops 15032385536 | bytes 88080384 | tf_op jit(solution)/shard_map/pallas_call | solution.py:348
  123.4 1.6 %copy.20 = bf16[64,1792]{1,0:T(8,128)(2,1)} copy(bf16[64,1792]{1,0:T(8,128)(2,1)} %shard_map.122) | data formatting | bytes 458752
  (5 shorter events, 0.0 us)

commit v2 on v1

--- a/solution.py
+++ b/solution.py
@@ -57,11 +57,12 @@
 VMEM_LIMIT = 62 * 1024 * 1024
 
 
-def fits_kernel(tokens, w_gate):
+def fits_kernel(w_gate, latent):
     return (
         lax.axis_size("role") == 4
         and lax.axis_size("expert") * MOST <= 128
         and w_gate.shape[0] >= DOWN_SLOTS
+        and latent.shape[0] == BLK
     )
 
 
@@ -73,7 +74,10 @@
     wg_ref,
     wu_ref,
     wd_ref,
+    rows_ref,
+    source_ref,
     out_ref,
+    decode_ref,
     tok_all,
     info_all,
     info_mine,
@@ -105,6 +109,9 @@
     h_recv,
     p_send,
     p_recv,
+    cache_all,
+    c_send,
+    c_recv,
 ):
     z = lax.axis_index("expert")
     role = lax.axis_index("role")
@@ -158,6 +165,17 @@
 
     def info_copy(d):
         return remote(info_mine, info_all.at[d], info_send.at[d], info_recv.at[d], peers[d - 1])
+
+    def block_copy(kind):
+        place = cache_all.at[z, chip if kind < 2 else 1 - chip, core]
+        peer = chip_peer if kind == 0 else core_peer
+        return remote(place, place, c_send.at[kind], c_recv.at[kind], peer)
+
+    def span_copy(d):
+        place = cache_all.at[z]
+        return remote(place, place, c_send.at[2 + d], c_recv.at[2 + d], peers[d - 1])
+
+    cache_all[z, chip, core] = rows_ref[...]
 
     expert_id = lax.broadcasted_iota(jnp.int32, (EXPERTS, count), 0)
     member = jnp.zeros((EXPERTS, count), jnp.float32)
@@ -181,6 +199,8 @@
         info_copy(d).start()
     for d in range(1, sources):
         token_copy(d).start()
+    block_copy(0).start()
+    block_copy(1).start()
     tok_all[0:count, :] = tok_ref[...]
     for d in range(1, sources):
         info_copy(d).wait_recv()
@@ -280,14 +300,10 @@
         down_copy(e).wait()
         slot = lax.rem(e, DOWN_SLOTS)
 
-        def columns(j, carry):
-            cols = pl.ds(pl.multiple_of(j * 256, 256), 256)
-            acc[:, cols] += jnp.dot(
-                hs[...], dslots[slot, :, cols], preferred_element_type=jnp.float32
+        for j in range(0, width, 256):
+            acc[:, j : j + 256] += jnp.dot(
+                hs[...], dslots[slot, :, j : j + 256], preferred_element_type=jnp.float32
             )
-            return carry
-
-        lax.fori_loop(0, width // 256, columns, 0)
 
         @pl.when(e + DOWN_SLOTS < experts)
         def _():
@@ -301,6 +317,18 @@
             @pl.when((i >= lag) & (i - lag < experts))
             def _():
                 stage(i - lag)
+
+        @pl.when(i == 1)
+        def _():
+            block_copy(0).wait_recv()
+            block_copy(2).start()
+
+        @pl.when(i == 3)
+        def _():
+            block_copy(1).wait_recv()
+            block_copy(2).wait_recv()
+            for d in range(1, sources):
+                span_copy(d).start()
 
         return carry
 
@@ -314,6 +342,12 @@
     for d in range(1, sources):
         psend[d] = acc[d * count : (d + 1) * count, :].astype(jnp.bfloat16)
         back_copy(d).start()
+    for d in range(1, sources):
+        span_copy(d).wait_recv()
+    block = source_ref[0]
+    decode_ref[...] = cache_all[
+        lax.div(block, 4), lax.rem(lax.div(block, 2), 2), lax.rem(block, 2)
+    ]
     total = acc[0:count, :]
     for d in range(1, sources):
         back_copy(d).wait_recv()
@@ -324,6 +358,9 @@
         info_copy(d).wait_send()
         token_copy(d).wait_send()
         back_copy(d).wait_send()
+        span_copy(d).wait_send()
+    for kind in range(3):
+        block_copy(kind).wait_send()
 
     def drain(e, carry):
         core_copy(e).wait_send()
@@ -335,7 +372,7 @@
     lax.fori_loop(0, experts, drain, 0)
 
 
-def experts_kernel(tokens, routes, route_weights, w_gate, w_up, w_down):
+def fused_kernel(tokens, routes, route_weights, w_gate, w_up, w_down, rows, slot_source):
     sources = lax.axis_size("expert")
     count, width = tokens.shape
     experts, _, ff = w_gate.shape
@@ -347,9 +384,12 @@
     dma = pltpu.SemaphoreType.DMA
     return pl.pallas_call(
         functools.partial(moe_kernel, sources),
-        out_shape=jax.ShapeDtypeStruct((count, width), bf16),
-        in_specs=[vmem, vmem, vmem, hbm, hbm, hbm],
-        out_specs=vmem,
+        out_shape=(
+            jax.ShapeDtypeStruct((count, width), bf16),
+            jax.ShapeDtypeStruct(rows.shape, bf16),
+        ),
+        in_specs=[vmem, vmem, vmem, hbm, hbm, hbm, vmem, pl.BlockSpec(memory_space=pltpu.SMEM)],
+        out_specs=(vmem, vmem),
         scratch_shapes=[
             pltpu.VMEM((sources * count, width), bf16),
             pltpu.VMEM((sources, 2 * EXPERTS, 128), f32),
@@ -382,6 +422,9 @@
             dma((experts, 3)),
             dma((sources,)),
             dma((sources,)),
+            pltpu.VMEM((sources, 2, 2) + rows.shape, bf16),
+            dma((2 + sources,)),
+            dma((2 + sources,)),
         ],
         compiler_params=pltpu.CompilerParams(
             collective_id=0, has_side_effects=True, vmem_limit_bytes=VMEM_LIMIT
@@ -391,7 +434,7 @@
             bytes_accessed=6 * experts * width * ff,
             transcendentals=0,
         ),
-    )(tokens, routes.T, route_weights.T, w_gate, w_up, w_down)
+    )(tokens, routes.T, route_weights.T, w_gate, w_up, w_down, rows, slot_source)
 
 
 def experts_plain(tokens, routes, route_weights, w_gate, w_up, w_down):
@@ -431,14 +474,17 @@
     return mixed_out
 
 
-def decode_blocks(latent, norm_gain, prompt_lengths, span_offsets, slot_source):
+def span_rows(latent, norm_gain, prompt_lengths, span_offsets):
     latent_count = latent.shape[0]
     token_index = lax.axis_index(("expert", "role")) * latent_count + jnp.arange(
         latent_count, dtype=jnp.int32
     )
     positions_f = token_positions(token_index, prompt_lengths, span_offsets)
-    cache_rows = latent_rows(latent, norm_gain, positions_f)
-    blocks = cache_rows.reshape(latent_count // BLK, BLK * latent.shape[1])
+    return latent_rows(latent, norm_gain, positions_f)
+
+
+def decode_plain(cache_rows, slot_source):
+    blocks = cache_rows.reshape(-1, BLK * cache_rows.shape[1])
     shard_piece = lax.all_gather(blocks, ("expert", "role"), axis=0, tiled=True)
     block_ids = jnp.arange(shard_piece.shape[0], dtype=jnp.int32)
     picker = (slot_source[:, None] == block_ids[None, :]).astype(jnp.bfloat16)
@@ -461,11 +507,15 @@
     span_offsets,
     slot_source,
 ):
-    decode_cache = decode_blocks(latent, norm_gain, prompt_lengths, span_offsets, slot_source)
-    if fits_kernel(tokens, w_gate):
-        mixed_out = experts_kernel(tokens, routes, route_weights, w_gate, w_up, w_down)
+    rows = span_rows(latent, norm_gain, prompt_lengths, span_offsets)
+    if fits_kernel(w_gate, latent):
+        mixed_out, block = fused_kernel(
+            tokens, routes, route_weights, w_gate, w_up, w_down, rows, slot_source
+        )
+        decode_cache = block.reshape(1, -1)
     else:
         mixed_out = experts_plain(tokens, routes, route_weights, w_gate, w_up, w_down)
+        decode_cache = decode_plain(rows, slot_source)
     return (mixed_out, decode_cache)
 
 

time: 125 us -> 104 us (0.83)
  blocking collectives: 24.8 us -> 0 us
  Pallas kernels: 92.2 us -> 94.5 us
    all_gather x1 -> x0, blocking collectives: 24.8 us -> none  [decode_blocks(): shard_piece = lax.all_gather(blocks, ('expert', 'role'), axis=0, tiled=True)]
    pallas_call x1, Pallas kernels: 92.2 us -> 94.5 us  [fused_kernel(): pl.pallas_call(functools.partial(moe_kernel, sources), out_shape=(jax.Sha...]
    reshape x0 -> x1, local copies, waits for them, and re-layouts: none -> 1.44 us  [local(): decode_cache = block.reshape(1, -1)]
where the time goes in v2:
time: 104 us
  Pallas kernels  94.5 us (91%)
  other arithmetic  4.68 us (4%)
  local copies, waits for them, and re-layouts  3.08 us (3%)
  between operations  1.31 us (1%)
    pallas_call x1, Pallas kernels, fused_kernel(): pl.pallas_call(functools.partial(moe_kernel, sources), out_shape=(jax.Sha...  94.5 us

profile of v2, /device:TPU:0, one launch (start us, length us, event | category | flops | bytes accessed | tf_op | source)
XLA Modules:
  0.0 103.6 jit_solution(8914176715538081616)
XLA Ops:
  1.3 0.8 reduce-window.8
  2.1 0.7 bitcast_subtract_fusion
  2.8 0.7 select_reduce_fusion
  3.5 0.7 convert_element_type.11
  4.3 0.1 multiply_reduce_fusion
  4.4 0.1 fusion.5
  4.5 0.8 multiply_convert_fusion
  5.3 0.7 pad_maximum_fusion.rows_ref
  6.0 94.5 %shard_map.122 = (bf16[64,1792]{1,0:T(8,128)(2,1)}, bf16[16,576]{1,0:T(8,128)(2,1)}) custom-call(bf16[64,1792]{1,0:T(8,128)(2,1)} %tok_ref.1, s32[8,64]{1,0:T(8,128)} %bitcast.5, f32[8,64]{1,0:T(8,128)} %bitcast.6, bf16[8,1792,1024]{2,1,0:T(8,128)(2,1)} %wg_ref.1, bf16[8,1792,1024]{2,1,0:T(8,128)(2,1)} %wu_ref.1, bf16[8,1024,1792]{2,1,0:T(8,128)(2,1)} %wd_ref.1, ...), custom_call_target="tpu_custom_call" | custom-call | flops 15032385536 | bytes 88080384 | tf_op jit(solution)/shard_map/pallas_call | solution.py:385
  100.5 1.4 %reshape.55 = bf16[1,9216]{1,0:T(2,128)(2,1)} reshape(bf16[16,576]{1,0:T(8,128)(2,1)} %get-tuple-element.5) | data formatting | bytes 36864 | tf_op jit(solution)/shard_map/reshape | solution.py:515
  102.0 1.6 %copy.15 = bf16[64,1792]{1,0:T(8,128)(2,1)} copy(bf16[64,1792]{1,0:T(8,128)(2,1)} %get-tuple-element.10) | data formatting | bytes 458752
  (4 shorter events, 0.0 us)

commit v3 on v2

--- a/solution.py
+++ b/solution.py
@@ -3,6 +3,7 @@
 
 import jax
 import jax.numpy as jnp
+import numpy as np
 from jax import lax
 from jax.experimental import pallas as pl
 from jax.experimental.pallas import tpu as pltpu
@@ -57,30 +58,33 @@
 VMEM_LIMIT = 62 * 1024 * 1024
 
 
-def fits_kernel(w_gate, latent):
+def fits_kernel(tokens, w_gate, latent):
     return (
         lax.axis_size("role") == 4
         and lax.axis_size("expert") * MOST <= 128
         and w_gate.shape[0] >= DOWN_SLOTS
         and latent.shape[0] == BLK
+        and 2 * tokens.shape[0] == 128
     )
 
 
 def moe_kernel(
     sources,
     tok_ref,
-    routes_ref,
-    rw_ref,
+    info_ref,
     wg_ref,
     wu_ref,
     wd_ref,
-    rows_ref,
+    latent_ref,
+    gain_ref,
+    freq_ref,
+    lengths_ref,
+    offsets_ref,
     source_ref,
     out_ref,
     decode_ref,
     tok_all,
     info_all,
-    info_mine,
     info_row,
     wslots,
     dslots,
@@ -158,13 +162,29 @@
             device_id_type=pl.DeviceIdType.MESH,
         )
 
-    def token_copy(d):
+    onward = ({"expert": lax.min(z + 1, sources - 1)}, {"expert": lax.max(z - 1, 0)})
+
+    def sends(way, k):
+        return (z - k >= 0) & (z < sources - 1) if way == 0 else (z + k < sources) & (z > 0)
+
+    def gets(way, k):
+        return z - 1 - k >= 0 if way == 0 else z + 1 + k < sources
+
+    def at_end(way):
+        return z == sources - 1 if way == 0 else z == 0
+
+    def token_hop(way, k, arriving=False):
+        back = k + 1 if arriving else k
+        block = jnp.clip(z - back if way == 0 else z + back, 0, sources - 1)
+        place = tok_all.at[pl.ds(pl.multiple_of(block * count, count), count)]
+        src = tok_ref if k == 0 and not arriving else place
+        return remote(src, place, tok_send.at[way, k], tok_recv.at[way, k], onward[way])
+
+    def info_copy(d, arriving=False):
+        place = info_all.at[lax.rem(z + sources - d, sources) if arriving else z]
         return remote(
-            tok_ref, tok_all.at[pl.ds(d * count, count)], tok_send.at[d], tok_recv.at[d], peers[d - 1]
+            place if arriving else info_ref, place, info_send.at[d], info_recv.at[d], peers[d - 1]
         )
-
-    def info_copy(d):
-        return remote(info_mine, info_all.at[d], info_send.at[d], info_recv.at[d], peers[d - 1])
 
     def block_copy(kind):
         place = cache_all.at[z, chip if kind < 2 else 1 - chip, core]
@@ -175,42 +195,83 @@
         place = cache_all.at[z]
         return remote(place, place, c_send.at[2 + d], c_recv.at[2 + d], peers[d - 1])
 
-    cache_all[z, chip, core] = rows_ref[...]
-
-    expert_id = lax.broadcasted_iota(jnp.int32, (EXPERTS, count), 0)
-    member = jnp.zeros((EXPERTS, count), jnp.float32)
-    weight = jnp.zeros((EXPERTS, count), jnp.float32)
-    for k in range(routes_ref.shape[0]):
-        hit = routes_ref[k : k + 1, :] == expert_id
-        member = member + jnp.where(hit, 1.0, 0.0)
-        weight = weight + jnp.where(hit, rw_ref[k : k + 1, :], 0.0)
-    before = jnp.where(
-        lax.broadcasted_iota(jnp.int32, (count, count), 0)
-        < lax.broadcasted_iota(jnp.int32, (count, count), 1),
-        1.0,
-        0.0,
-    ).astype(jnp.bfloat16)
-    rank = jnp.dot(member.astype(jnp.bfloat16), before, preferred_element_type=jnp.float32)
-    info_mine[0:EXPERTS, 0:count] = jnp.where(member > 0.5, rank, -1000.0)
-    info_mine[EXPERTS : 2 * EXPERTS, 0:count] = weight
-    info_mine[:, count:] = jnp.zeros((2 * EXPERTS, info_mine.shape[1] - count), jnp.float32)
-
     for d in range(1, sources):
         info_copy(d).start()
-    for d in range(1, sources):
-        token_copy(d).start()
+    for way in range(2):
+
+        @pl.when(sends(way, 0))
+        def _():
+            token_hop(way, 0).start()
+
+    tok_all[pl.ds(pl.multiple_of(z * count, count), count), :] = tok_ref[...]
+    info_all[z] = info_ref[...]
+    acc[...] = jnp.zeros_like(acc)
+
+    span_rows_here = latent_ref.shape[0]
+    at = (z * 4 + role) * span_rows_here + lax.broadcasted_iota(jnp.int32, (span_rows_here, 1), 0)
+    position = jnp.zeros((span_rows_here, 1), jnp.int32)
+    start = jnp.int32(0)
+    for p in range(lengths_ref.shape[0]):
+        stop = start + lengths_ref[p]
+        position += jnp.where((at >= start) & (at < stop), offsets_ref[p] + at - start, 0)
+        start = stop
+    angle = position.astype(jnp.float32) * freq_ref[...]
+    turns = jnp.floor(angle * (0.5 / math.pi) + 0.5)
+    angle = (angle - turns * 6.28125) - turns * (2.0 * math.pi - 6.28125)
+    cosine, sine = jnp.cos(angle), jnp.sin(angle)
+    latent_f = latent_ref[...].astype(jnp.float32)
+    compressed = latent_f[:, :LAT]
+    mean_square = jnp.mean(compressed * compressed, axis=1, keepdims=True)
+    normed = compressed * lax.rsqrt(mean_square + 1e-06) * gain_ref[...]
+    first = latent_f[:, LAT : LAT + ROPE // 2]
+    second = latent_f[:, LAT + ROPE // 2 :]
+    rotated = jnp.concatenate(
+        [first * cosine - second * sine, second * cosine + first * sine], axis=1
+    )
+    cache_all[z, chip, core, :, :LAT] = normed.astype(jnp.bfloat16)
+    cache_all[z, chip, core, :, LAT:] = rotated.astype(jnp.bfloat16)
     block_copy(0).start()
     block_copy(1).start()
-    tok_all[0:count, :] = tok_ref[...]
+
     for d in range(1, sources):
-        info_copy(d).wait_recv()
-    rows = [info_mine[:, 0:count]] + [info_all[d, :, 0:count] for d in range(1, sources)]
-    rows = [r + jnp.where(
-        lax.broadcasted_iota(jnp.int32, r.shape, 0) < EXPERTS, float(d * MOST), 0.0
-    ) for d, r in enumerate(rows)]
-    info_row[...] = jnp.concatenate(rows, axis=1)
-    for d in range(1, sources):
-        token_copy(d).wait_recv()
+        info_copy(d, True).wait_recv()
+    named = jnp.concatenate([info_all[s, :, :count] for s in range(sources)], axis=1)
+    weights = jnp.concatenate([info_all[s, :, count : 2 * count] for s in range(sources)], axis=1)
+    total_tokens = sources * count
+    expert_id = lax.broadcasted_iota(jnp.int32, (EXPERTS, total_tokens), 0).astype(jnp.float32)
+    member = jnp.zeros((EXPERTS, total_tokens), jnp.float32)
+    weight = jnp.zeros((EXPERTS, total_tokens), jnp.float32)
+    for k in range(info_ref.shape[0]):
+        hit = named[k : k + 1, :] == expert_id
+        member = member + jnp.where(hit, 1.0, 0.0)
+        weight = weight + jnp.where(hit, weights[k : k + 1, :], 0.0)
+    earlier = lax.broadcasted_iota(jnp.int32, (total_tokens, total_tokens), 0)
+    later = lax.broadcasted_iota(jnp.int32, (total_tokens, total_tokens), 1)
+    before = (earlier < later) & (lax.div(earlier, count) == lax.div(later, count))
+    rank = jnp.dot(
+        member.astype(jnp.bfloat16),
+        jnp.where(before, 1.0, 0.0).astype(jnp.bfloat16),
+        preferred_element_type=jnp.float32,
+    )
+    source = lax.div(lax.broadcasted_iota(jnp.int32, (EXPERTS, total_tokens), 1), count)
+    first_slot = (source * MOST).astype(jnp.float32)
+    info_row[0:EXPERTS, :] = jnp.where(member > 0.5, rank + first_slot, -1.0)
+    info_row[EXPERTS : 2 * EXPERTS, :] = weight
+
+    for k in range(1, sources - 1):
+        for way in range(2):
+
+            @pl.when(sends(way, k))
+            def _():
+                token_hop(way, k - 1, True).wait_recv()
+                token_hop(way, k).start()
+
+    for k in range(sources - 1):
+        for way in range(2):
+
+            @pl.when(gets(way, k) & at_end(way))
+            def _():
+                token_hop(way, k, True).wait_recv()
 
     slot_id = lax.broadcasted_iota(jnp.int32, (slots, sources * count), 0).astype(jnp.float32)
 
@@ -309,8 +370,6 @@
         def _():
             down_copy(e + DOWN_SLOTS).start()
 
-    acc[...] = jnp.zeros_like(acc)
-
     def step(i, carry):
         for lag, stage in enumerate((project, add_core, activate, forward, finish)):
 
@@ -334,31 +393,68 @@
 
     lax.fori_loop(0, experts + 4, step, 0)
 
-    def back_copy(d):
+    def back_hop(way, b):
         return remote(
-            psend.at[d], precv.at[d], p_send.at[d], p_recv.at[d], {"expert": lax.rem(z + sources - d, sources)}
+            psend.at[way, b], precv.at[way, b], p_send.at[way, b], p_recv.at[way, b], onward[way]
         )
 
-    for d in range(1, sources):
-        psend[d] = acc[d * count : (d + 1) * count, :].astype(jnp.bfloat16)
-        back_copy(d).start()
+    def passes(way, b):
+        return z < b if way == 0 else z > b
+
+    def hand_on(way, b):
+        @pl.when(passes(way, b))
+        def _():
+            rows = slice(b * count, (b + 1) * count)
+
+            @pl.when(gets(way, 0))
+            def _():
+                back_hop(way, b).wait_recv()
+                psend[way, b] = (acc[rows, :] + precv[way, b].astype(jnp.float32)).astype(
+                    jnp.bfloat16
+                )
+
+            @pl.when(jnp.logical_not(gets(way, 0)))
+            def _():
+                psend[way, b] = acc[rows, :].astype(jnp.bfloat16)
+
+            back_hop(way, b).start()
+
+    for step_back in range(sources - 1):
+        hand_on(0, sources - 1 - step_back)
+        hand_on(1, step_back)
+
     for d in range(1, sources):
         span_copy(d).wait_recv()
     block = source_ref[0]
     decode_ref[...] = cache_all[
         lax.div(block, 4), lax.rem(lax.div(block, 2), 2), lax.rem(block, 2)
     ]
-    total = acc[0:count, :]
-    for d in range(1, sources):
-        back_copy(d).wait_recv()
-        total = total + precv[d].astype(jnp.float32)
-    out_ref[...] = total.astype(out_ref.dtype)
+    mine_rows = pl.ds(pl.multiple_of(z * count, count), count)
+    for way in range(2):
+
+        @pl.when(gets(way, 0))
+        def _():
+            back_hop(way, z).wait_recv()
+            acc[mine_rows, :] += precv[way, z].astype(jnp.float32)
+
+    out_ref[...] = acc[mine_rows, :].astype(out_ref.dtype)
 
     for d in range(1, sources):
         info_copy(d).wait_send()
-        token_copy(d).wait_send()
-        back_copy(d).wait_send()
         span_copy(d).wait_send()
+    for way in range(2):
+        for k in range(sources - 1):
+
+            @pl.when(sends(way, k))
+            def _():
+                token_hop(way, k).wait_send()
+
+        for b in range(sources):
+
+            @pl.when(passes(way, b))
+            def _():
+                back_hop(way, b).wait_send()
+
     for kind in range(3):
         block_copy(kind).wait_send()
 
@@ -372,28 +468,43 @@
     lax.fori_loop(0, experts, drain, 0)
 
 
-def fused_kernel(tokens, routes, route_weights, w_gate, w_up, w_down, rows, slot_source):
+def fused_kernel(
+    tokens,
+    routes,
+    route_weights,
+    w_gate,
+    w_up,
+    w_down,
+    latent,
+    norm_gain,
+    prompt_lengths,
+    span_offsets,
+    slot_source,
+):
     sources = lax.axis_size("expert")
     count, width = tokens.shape
     experts, _, ff = w_gate.shape
     slots = sources * MOST
     half, quarter = ff // 2, ff // 4
     bf16, f32 = jnp.bfloat16, jnp.float32
+    info = jnp.concatenate([routes.T.astype(f32), route_weights.T], axis=1)
+    half_rope = ROPE // 2
+    freq = 10000.0 ** (-2.0 * np.arange(half_rope) / ROPE)
     vmem = pl.BlockSpec(memory_space=pltpu.VMEM)
+    smem = pl.BlockSpec(memory_space=pltpu.SMEM)
     hbm = pl.BlockSpec(memory_space=pl.ANY)
     dma = pltpu.SemaphoreType.DMA
     return pl.pallas_call(
         functools.partial(moe_kernel, sources),
         out_shape=(
             jax.ShapeDtypeStruct((count, width), bf16),
-            jax.ShapeDtypeStruct(rows.shape, bf16),
+            jax.ShapeDtypeStruct(latent.shape, bf16),
         ),
-        in_specs=[vmem, vmem, vmem, hbm, hbm, hbm, vmem, pl.BlockSpec(memory_space=pltpu.SMEM)],
+        in_specs=[vmem, vmem, hbm, hbm, hbm, vmem, vmem, vmem, smem, smem, smem],
         out_specs=(vmem, vmem),
         scratch_shapes=[
             pltpu.VMEM((sources * count, width), bf16),
-            pltpu.VMEM((sources, 2 * EXPERTS, 128), f32),
-            pltpu.VMEM((2 * EXPERTS, 128), f32),
+            pltpu.VMEM((sources,) + info.shape, f32),
             pltpu.VMEM((2 * EXPERTS, sources * count), f32),
             pltpu.VMEM((GATE_SLOTS, width, ff), bf16),
             pltpu.VMEM((DOWN_SLOTS, ff, width), bf16),
@@ -406,12 +517,12 @@
             pltpu.VMEM((experts, 4, slots, quarter), bf16),
             pltpu.VMEM((sources * count, ff), bf16),
             pltpu.VMEM((sources * count, width), f32),
-            pltpu.VMEM((sources, count, width), bf16),
-            pltpu.VMEM((sources, count, width), bf16),
+            pltpu.VMEM((2, sources, count, width), bf16),
+            pltpu.VMEM((2, sources, count, width), bf16),
             dma((GATE_SLOTS,)),
             dma((DOWN_SLOTS,)),
-            dma((sources,)),
-            dma((sources,)),
+            dma((2, sources)),
+            dma((2, sources)),
             dma((sources,)),
             dma((sources,)),
             dma((experts,)),
@@ -420,9 +531,9 @@
             dma((experts,)),
             dma((experts, 3)),
             dma((experts, 3)),
-            dma((sources,)),
-            dma((sources,)),
-            pltpu.VMEM((sources, 2, 2) + rows.shape, bf16),
+            dma((2, sources)),
+            dma((2, sources)),
+            pltpu.VMEM((sources, 2, 2) + latent.shape, bf16),
             dma((2 + sources,)),
             dma((2 + sources,)),
         ],
@@ -434,7 +545,19 @@
             bytes_accessed=6 * experts * width * ff,
             transcendentals=0,
         ),
-    )(tokens, routes.T, route_weights.T, w_gate, w_up, w_down, rows, slot_source)
+    )(
+        tokens,
+        info,
+        w_gate,
+        w_up,
+        w_down,
+        latent,
+        norm_gain[None, :],
+        jnp.asarray(freq[None, :], f32),
+        prompt_lengths,
+        span_offsets,
+        slot_source,
+    )
 
 
 def experts_plain(tokens, routes, route_weights, w_gate, w_up, w_down):
@@ -507,14 +630,24 @@
     span_offsets,
     slot_source,
 ):
-    rows = span_rows(latent, norm_gain, prompt_lengths, span_offsets)
-    if fits_kernel(w_gate, latent):
+    if fits_kernel(tokens, w_gate, latent):
         mixed_out, block = fused_kernel(
-            tokens, routes, route_weights, w_gate, w_up, w_down, rows, slot_source
+            tokens,
+            routes,
+            route_weights,
+            w_gate,
+            w_up,
+            w_down,
+            latent,
+            norm_gain,
+            prompt_lengths,
+            span_offsets,
+            slot_source,
         )
         decode_cache = block.reshape(1, -1)
     else:
         mixed_out = experts_plain(tokens, routes, route_weights, w_gate, w_up, w_down)
+        rows = span_rows(latent, norm_gain, prompt_lengths, span_offsets)
         decode_cache = decode_plain(rows, slot_source)
     return (mixed_out, decode_cache)
 

time: 104 us -> 101 us (0.971)
  other arithmetic: 4.68 us -> 2.04 us
    another operation x3 -> x0, other arithmetic: 1.72 us -> none
where the time goes in v3:
time: 101 us
  Pallas kernels  94.7 us (94%)
  local copies, waits for them, and re-layouts  3.08 us (3%)
  other arithmetic  2.04 us (2%)
  between operations  1.29 us (1%)
    pallas_call x1, Pallas kernels, fused_kernel(): pl.pallas_call(functools.partial(moe_kernel, sources), out_shape=(jax.Sha...  94.7 us

profile of v3, /device:TPU:0, one launch (start us, length us, event | category | flops | bytes accessed | tf_op | source)
XLA Modules:
  0.0 101.1 jit_solution(15347456700985288758)
XLA Ops:
  1.3 0.7 convert_bitcast_fusion
  2.0 1.4 %pad_maximum_fusion.info_ref = f32[8,128]{1,0:T(8,128)} fusion(f32[8,64]{1,0:T(8,128)} %bitcast.4, f32[8,64]{1,0:T(8,128)S(1)} %convert_bitcast_fusion), kind=kLoop, calls=%fused_computation | loop fusion | flops 1024 | bytes 8192 | tf_op jit(solution)/shard_map/concatenate | solution.py:490
  3.3 94.7 %shard_map.131 = (bf16[64,1792]{1,0:T(8,128)(2,1)}, bf16[16,576]{1,0:T(8,128)(2,1)}) custom-call(bf16[64,1792]{1,0:T(8,128)(2,1)} %tok_ref.1, f32[8,128]{1,0:T(8,128)} %pad_maximum_fusion.info_ref, bf16[8,1792,1024]{2,1,0:T(8,128)(2,1)} %wg_ref.1, bf16[8,1792,1024]{2,1,0:T(8,128)(2,1)} %wu_ref.1, bf16[8,1024,1792]{2,1,0:T(8,128)(2,1)} %wd_ref.1, ...), custom_call_target="tpu_custom_call" | custom-call | flops 15032385536 | bytes 88080384 | tf_op jit(solution)/shard_map/pallas_call | solution.py:497
  98.0 1.4 %reshape.7 = bf16[1,9216]{1,0:T(2,128)(2,1)} reshape(bf16[16,576]{1,0:T(8,128)(2,1)} %get-tuple-element.5) | data formatting | bytes 36864 | tf_op jit(solution)/shard_map/reshape | solution.py:647
  99.5 1.6 %copy.16 = bf16[64,1792]{1,0:T(8,128)(2,1)} copy(bf16[64,1792]{1,0:T(8,128)(2,1)} %get-tuple-element.8) | data formatting | bytes 458752

commit v4 on v3

--- a/solution.py
+++ b/solution.py
@@ -371,7 +371,8 @@
             down_copy(e + DOWN_SLOTS).start()
 
     def step(i, carry):
-        for lag, stage in enumerate((project, add_core, activate, forward, finish)):
+        stages = ((0, project), (1, add_core), (3, activate), (5, forward), (6, finish))
+        for lag, stage in stages:
 
             @pl.when((i >= lag) & (i - lag < experts))
             def _():
@@ -391,7 +392,7 @@
 
         return carry
 
-    lax.fori_loop(0, experts + 4, step, 0)
+    lax.fori_loop(0, experts + 6, step, 0)
 
     def back_hop(way, b):
         return remote(

time: 101 us -> 100 us (0.990)
  Pallas kernels: 94.7 us -> 93.5 us
    pallas_call x1, Pallas kernels: 94.7 us -> 93.5 us  [fused_kernel(): pl.pallas_call(functools.partial(moe_kernel, sources), out_shape=(jax.Sha...]
where the time goes in v4:
time: 100 us; the launch traced here: 99.9 us
  Pallas kernels  93.5 us (94%)
  local copies, waits for them, and re-layouts  3.08 us (3%)
  other arithmetic  2.04 us (2%)
  between operations  1.29 us (1%)
    pallas_call x1, Pallas kernels, fused_kernel(): pl.pallas_call(functools.partial(moe_kernel, sources), out_shape=(jax.Sha...  93.5 us

profile of v4, /device:TPU:0, one launch (start us, length us, event | category | flops | bytes accessed | tf_op | source)
XLA Modules:
  0.0 99.9 jit_solution(5802530491391214775)
XLA Ops:
  1.3 0.7 convert_bitcast_fusion
  2.0 1.4 %pad_maximum_fusion.info_ref = f32[8,128]{1,0:T(8,128)} fusion(f32[8,64]{1,0:T(8,128)} %bitcast.4, f32[8,64]{1,0:T(8,128)S(1)} %convert_bitcast_fusion), kind=kLoop, calls=%fused_computation | loop fusion | flops 1024 | bytes 8192 | tf_op jit(solution)/shard_map/concatenate | solution.py:491
  3.3 93.5 %shard_map.131 = (bf16[64,1792]{1,0:T(8,128)(2,1)}, bf16[16,576]{1,0:T(8,128)(2,1)}) custom-call(bf16[64,1792]{1,0:T(8,128)(2,1)} %tok_ref.1, f32[8,128]{1,0:T(8,128)} %pad_maximum_fusion.info_ref, bf16[8,1792,1024]{2,1,0:T(8,128)(2,1)} %wg_ref.1, bf16[8,1792,1024]{2,1,0:T(8,128)(2,1)} %wu_ref.1, bf16[8,1024,1792]{2,1,0:T(8,128)(2,1)} %wd_ref.1, ...), custom_call_target="tpu_custom_call" | custom-call | flops 15032385536 | bytes 88080384 | tf_op jit(solution)/shard_map/pallas_call | solution.py:498
  96.8 1.4 %reshape.7 = bf16[1,9216]{1,0:T(2,128)(2,1)} reshape(bf16[16,576]{1,0:T(8,128)(2,1)} %get-tuple-element.5) | data formatting | bytes 36864 | tf_op jit(solution)/shard_map/reshape | solution.py:648
  98.3 1.6 %copy.16 = bf16[64,1792]{1,0:T(8,128)(2,1)} copy(bf16[64,1792]{1,0:T(8,128)(2,1)} %get-tuple-element.8) | data formatting | bytes 458752
